TPU v7x, 32 devices: a whole 2x2x4 slice. The times are simulated.
32 devices in a mesh: dp: 4 (over y, x), dict: 8 (over z, core).
Axes of the slice: x: 2, y: 2, z: 4, core: 2. Of those that a mesh axis runs over, the one named last changes fastest.
Arguments:
- acts: bfloat16 [2048, 8192], P('dict', 'dp'), may hold values from -6 to 6
- lists: int32 [128, 2], P('dict'), may hold values from 0 to 7, all different within a row; in each aligned block of 16 rows (0 to 15, 16 to 31, ...) at most 8 rows name the same one
- w_enc: bfloat16 [8192, 8192], P('dp', 'dict'), may hold values from -0.0625 to 0.0625
- w_dec: bfloat16 [8192, 8192], P('dict', 'dp'), may hold values from -0.1875 to 0.1875
- b_enc: bfloat16 [8192], P('dict'), may hold values from -3 to 3
- b_dec: bfloat16 [8192], P('dp'), may hold values from -3 to 3
Outputs:
- grad_enc: bfloat16 [8192, 8192], P('dp', 'dict')
- grad_dec: bfloat16 [8192, 8192], P('dict', 'dp')
Inputs may be any that keep to these rules, and one draw needn't show every extreme that they name: Each row block lists 2 different panels. Among the 16 row blocks of one index of dict, no panel is listed by more than 8 blocks, and some panel is listed by exactly 8.
All inputs are finite; a program needn't handle non-finite values.
Results may differ from a plain program's by a relative error of at most 0.0057.
Values may be sent and summed in bfloat16 or wider, within the bound.
A program may use at most 128 MiB of HBM per device.

v0:
```python
import jax
import jax.numpy as jnp
from jax import lax
from jax.sharding import PartitionSpec as P


def on_device(acts, lists, w_enc, w_dec, b_enc, b_dec):
    peers = lax.axis_size("dict")
    block_count = lists.shape[0]
    active_count = lists.shape[1]
    rows_block = acts.shape[0] // block_count
    feature_cols = acts.shape[1]
    capacity = max(2, (2 * block_count * active_count + peers - 1) // peers)
    slot_total = peers * capacity
    flat_ids = lists.reshape(-1)
    onehot = (flat_ids[:, None] == jnp.arange(peers, dtype=jnp.int32)[None, :]).astype(jnp.int32)
    rank_index = jnp.sum((jnp.cumsum(onehot, axis=0) - 1) * onehot, axis=1)
    slot_index = flat_ids * capacity + rank_index
    item_block = jnp.arange(block_count * active_count, dtype=jnp.int32) // active_count
    slot_match = (jnp.arange(slot_total, dtype=jnp.int32)[:, None] == slot_index[None, :]).astype(
        jnp.float32
    )
    block_match = (item_block[:, None] == jnp.arange(block_count, dtype=jnp.int32)[None, :]).astype(
        jnp.float32
    )
    selector = jnp.dot(slot_match, block_match).astype(jnp.bfloat16)
    block_rows = acts.reshape(block_count, rows_block * feature_cols)
    outgoing = jnp.dot(selector, block_rows, preferred_element_type=jnp.float32).astype(
        jnp.bfloat16
    )
    outgoing = outgoing.reshape(peers, capacity * rows_block, feature_cols)
    received = lax.all_to_all(outgoing, "dict", split_axis=0, concat_axis=0, tiled=True)
    rows_in = received.reshape(-1, feature_cols)
    pre_local = jnp.dot(rows_in, w_enc, preferred_element_type=jnp.float32)
    bias_enc = b_enc.astype(jnp.float32)
    preact = lax.psum(pre_local, "dp") + bias_enc
    activity = (jnp.maximum(preact, 0.0) ** 2).astype(jnp.bfloat16)
    part = jnp.dot(activity, w_dec, preferred_element_type=jnp.float32).astype(jnp.bfloat16)
    part = part.reshape(peers, capacity * rows_block, feature_cols)
    returned = lax.all_to_all(part, "dict", split_axis=0, concat_axis=0, tiled=True)
    returned = returned.reshape(slot_total, rows_block * feature_cols)
    rebuilt = lax.dot_general(
        selector, returned, (((0,), (0,)), ((), ())), preferred_element_type=jnp.float32
    )
    rebuilt = rebuilt.reshape(block_count * rows_block, feature_cols) + b_dec.astype(jnp.float32)
    residual_g = ((rebuilt - acts.astype(jnp.float32)) * (1.0 / rows_block)).astype(jnp.bfloat16)
    resid_out = jnp.dot(
        selector,
        residual_g.reshape(block_count, rows_block * feature_cols),
        preferred_element_type=jnp.float32,
    ).astype(jnp.bfloat16)
    resid_out = resid_out.reshape(peers, capacity * rows_block, feature_cols)
    residual_in = lax.all_to_all(
        resid_out, "dict", split_axis=0, concat_axis=0, tiled=True
    ).reshape(-1, feature_cols)
    grad_dec = lax.dot_general(
        activity, residual_in, (((0,), (0,)), ((), ())), preferred_element_type=jnp.float32
    ).astype(jnp.bfloat16)
    dact_local = lax.dot_general(
        residual_in, w_dec, (((1,), (1,)), ((), ())), preferred_element_type=jnp.float32
    )
    dact = lax.psum(dact_local, "dp")
    grad_pre = (dact * 2.0 * jnp.maximum(preact, 0.0)).astype(jnp.bfloat16)
    grad_enc = lax.dot_general(
        rows_in, grad_pre, (((0,), (0,)), ((), ())), preferred_element_type=jnp.float32
    ).astype(jnp.bfloat16)
    return (grad_enc, grad_dec)


def solution(mesh):
    in_specs = (
        P("dict", "dp"),
        P("dict", None),
        P("dp", "dict"),
        P("dict", "dp"),
        P("dict"),
        P("dp"),
    )
    out_specs = (P("dp", "dict"), P("dict", "dp"))
    return jax.shard_map(
        on_device, mesh=mesh, in_specs=in_specs, out_specs=out_specs, check_vma=False
    )
```

profile of v0, /device:TPU:0, one launch (start us, length us, event | category | flops | bytes accessed | tf_op | source)
XLA Modules:
  0.0 594.1 jit_solution(12018734821339683445)
XLA Ops:
  7.2 0.0 all-reduce.3.cloned.1.call-start
  7.2 0.8 copy.9
  8.0 0.1 reshape.58
  8.1 0.1 fusion.4
  8.1 0.1 reduce_window_sum.11
  8.2 0.2 select_reduce_fusion
  8.4 1.6 reshape.59
  9.9 0.2 convolution_convert_fusion.5
  10.2 3.3 convolution_convert_fusion.1
  13.5 7.4 %reshape.60 = bf16[8,128,2048]{2,1,0:T(8,128)(2,1)} reshape(bf16[64,32768]{1,0:T(8,128)(2,1)} %convolution_convert_fusion.1) | data formatting | bytes 8388608 | tf_op jit(solution)/shard_map/reshape | solution.py:31
  20.9 0.0 copy-start.5
  20.9 100.6 %all_to_all.15 = bf16[8,128,2048]{2,1,0:T(8,128)(2,1)S(1)} all-to-all(bf16[8,128,2048]{2,1,0:T(8,128)(2,1)} %reshape.60), channel_id=1, replica_groups=mesh['dp'=4,'dict'=8] {'dict'}, dimensions={0} | all-to-all | bytes 8388608 | tf_op jit(solution)/shard_map/all_to_all | solution.py:32
  121.5 0.0 copy-start
  121.5 2.0 copy-done
  123.4 0.0 copy-done.5
  123.4 6.0 %fusion.10 = f32[1024,1024]{1,0:T(8,128)} fusion(bf16[1024,2048]{1,0:T(8,128)(2,1)S(1)} %bitcast.16, bf16[2048,1024]{1,0:T(8,128)(2,1)S(1)} %copy-done.5), kind=kOutput, calls=%fused_computation.29 | convolution fusion | flops 4294967296 | bytes 12582912 | tf_op jit(solution)/shard_map/dot_general | solution.py:34
  129.4 0.0 copy-start.4
  129.4 0.0 all-reduce.3.cloned.1.call-update
  129.5 0.7 copy-done.4
  130.1 102.2 %all-reduce.3.cloned.1.call-done = f32[1024,1024]{1,0:T(8,128)} async-done(((f32[1024,1024]{1,0:T(8,128)}), f32[1024,1024]{1,0:T(8,128)}) %all-reduce.3.cloned.1.call-update) | async-done | bytes 4194320 | tf_op jit(solution)/shard_map/psum | solution.py:36
  232.4 10.0 %convolution_convert_fusion.4 = bf16[1024,2048]{1,0:T(8,128)(2,1)} fusion(bf16[1024,2048]{1,0:T(8,128)(2,1)} %param.9, f32[1024,1024]{1,0:T(8,128)} %all-reduce.3.cloned.1.call-done, f32[1024]{0:T(1024)S(1)} %convert_element_type.44), kind=kOutput, calls=%fused_computation.7 | convolution fusion | flops 4301258752 | bytes 12587008 | tf_op jit(solution)/shard_map/dot_general | solution.py:38
  242.3 0.0 copy-start.3
  242.3 4.7 all-to-all-start.1
  247.1 0.0 all-reduce.5.cloned.1.call-start
  247.1 0.0 copy-done.3
  247.1 94.0 %all-to-all-done.1 = bf16[8,128,2048]{2,1,0:T(8,128)(2,1)} async-done(((bf16[8,128,2048]{2,1,0:T(8,128)(2,1)}), bf16[8,128,2048]{2,1,0:T(8,128)(2,1)}, u32[]{:S(2)}, u32[]{:S(2)}) %all-to-all-start.1) | async-done | bytes 4194336 | tf_op jit(solution)/shard_map/all_to_all | solution.py:40
  341.2 7.4 %reshape.63 = bf16[64,32768]{1,0:T(8,128)(2,1)} reshape(bf16[8,128,2048]{2,1,0:T(8,128)(2,1)} %all-to-all-done.1) | data formatting | bytes 8388608 | tf_op jit(solution)/shard_map/reshape | solution.py:41
  348.6 0.0 copy-start.2
  348.6 4.3 fusion.11
  352.8 1.7 reshape.64
  354.6 0.0 copy-done.2
  354.6 1.3 multiply_convert_fusion.3
  355.9 1.6 reshape.65
  357.5 3.3 convolution_convert_fusion
  360.7 7.4 %reshape.66 = bf16[8,128,2048]{2,1,0:T(8,128)(2,1)} reshape(bf16[64,32768]{1,0:T(8,128)(2,1)} %convolution_convert_fusion) | data formatting | bytes 8388608 | tf_op jit(solution)/shard_map/reshape | solution.py:52
  368.1 0.0 copy-start.6
  368.1 97.9 %all_to_all.16 = bf16[8,128,2048]{2,1,0:T(8,128)(2,1)S(1)} all-to-all(bf16[8,128,2048]{2,1,0:T(8,128)(2,1)} %reshape.66), channel_id=1, replica_groups=mesh['dp'=4,'dict'=8] {'dict'}, dimensions={0} | all-to-all | bytes 8388608 | tf_op jit(solution)/shard_map/all_to_all | solution.py:53
  466.0 0.0 copy-start.1
  466.0 1.9 copy-done.1
  467.9 0.0 copy-done.6
  467.9 6.1 %fusion.12 = f32[1024,1024]{1,0:T(8,128)} fusion(bf16[1024,2048]{1,0:T(8,128)(2,1)S(1)} %bitcast.18, bf16[1024,2048]{1,0:T(8,128)(2,1)S(1)} %copy-done.6), kind=kOutput, calls=%fused_computation.31 | convolution fusion | flops 4294967296 | bytes 12582912 | tf_op jit(solution)/shard_map/dot_general | solution.py:59
  474.0 0.0 all-reduce.5.cloned.1.call-update
  474.0 10.1 %convolution_convert_fusion.2 = bf16[1024,2048]{1,0:T(8,128)(2,1)} fusion(bf16[1024,2048]{1,0:T(8,128)(2,1)} %bitcast.19, f32[1024,1024]{1,0:T(8,128)} %all-reduce.3.cloned.1.call-done, f32[1024]{0:T(1024)S(1)} %convert_element_type.44), kind=kOutput, calls=%fused_computation.5 | convolution fusion | flops 4301258752 | bytes 12587008 | tf_op jit(solution)/shard_map/dot_general | solution.py:56
  484.1 91.8 %all-reduce.5.cloned.1.call-done = f32[1024,1024]{1,0:T(8,128)} async-done(((f32[1024,1024]{1,0:T(8,128)}), f32[1024,1024]{1,0:T(8,128)}) %all-reduce.5.cloned.1.call-update) | async-done | bytes 4194320 | tf_op jit(solution)/shard_map/psum | solution.py:62
  575.9 11.3 %convolution_convert_fusion.3 = bf16[2048,1024]{1,0:T(8,128)(2,1)} fusion(bf16[1024,2048]{1,0:T(8,128)(2,1)} %bitcast.17, f32[1024,1024]{1,0:T(8,128)} %all-reduce.5.cloned.1.call-done, f32[1024,1024]{1,0:T(8,128)} %all-reduce.3.cloned.1.call-done, f32[1024]{0:T(1024)S(1)} %convert_element_type.44), kind=kOutput, calls=%fused_computation.6 | convolution fusion | flops 4302307328 | bytes 16781312 | tf_op jit(solution)/shard_map/dot_general | solution.py:64
  (3 shorter events, 0.0 us)
Async XLA Ops:
  7.2 225.2 %all-reduce.3.cloned.1.call-start = ((), (), s32[]{:S(2)}) async-start(), calls=%async_computation.3 | async-start | bytes 8388608 | tf_op jit(solution)/shard_map/psum | solution.py:36
  20.9 102.6 %copy-start.5 = (bf16[2048,1024]{1,0:T(8,128)(2,1)S(1)}, bf16[2048,1024]{1,0:T(8,128)(2,1)}, u32[]{:S(2)}) copy-start(bf16[2048,1024]{1,0:T(8,128)(2,1)} %param.8) | copy-start | bytes 12582916
  121.5 2.0 copy-start
  129.4 0.7 copy-start.4
  242.3 4.8 copy-start.3
  242.3 98.9 %all-to-all-start.1 = ((bf16[8,128,2048]{2,1,0:T(8,128)(2,1)}), bf16[8,128,2048]{2,1,0:T(8,128)(2,1)}, u32[]{:S(2)}, u32[]{:S(2)}) async-start(bf16[8,128,2048]{2,1,0:T(8,128)(2,1)} %bitcast.20), calls=%async_computation.1 | async-start | bytes 8388608 | tf_op jit(solution)/shard_map/all_to_all | solution.py:40
  247.1 328.9 %all-reduce.5.cloned.1.call-start = ((), (), s32[]{:S(2)}) async-start(), calls=%async_computation.4 | async-start | bytes 8388608 | tf_op jit(solution)/shard_map/psum | solution.py:62
  348.6 6.0 %copy-start.2 = (bf16[256,2048]{1,0:T(8,128)(2,1)S(1)}, bf16[256,2048]{1,0:T(8,128)(2,1)}, u32[]{:S(2)}) copy-start(bf16[256,2048]{1,0:T(8,128)(2,1)} %param.6) | copy-start | bytes 3145732
  368.1 99.8 %copy-start.6 = (bf16[1024,2048]{1,0:T(8,128)(2,1)S(1)}, bf16[1024,2048]{1,0:T(8,128)(2,1)}, u32[]{:S(2)}) copy-start(bf16[1024,2048]{1,0:T(8,128)(2,1)} %param.9) | copy-start | bytes 12582916
  466.0 1.9 copy-start.1
Sparse Core Ops, SparseCore 0:
  129.6 102.7 all-reduce.2
  474.1 101.7 all-reduce.4
where the time goes:
time: 595 us; the launch traced here: 594 us
  waiting for transfers between devices  288 us (48%)
  blocking collectives  199 us (33%)
  matrix products  54.5 us (9%)
  local copies, waits for them, and re-layouts  32.4 us (5%)
  between operations  14.1 us (2%)
    psum x1, waiting for transfers between devices, on_device(): preact = lax.psum(pre_local, 'dp') + bias_enc  102 us
    all_to_all x1, blocking collectives, on_device(): lax.all_to_all(outgoing, 'dict', split_axis=0, concat_axis=0, tiled=True)  101 us
    all_to_all x1, blocking collectives, on_device(): lax.all_to_all(resid_out, 'dict', split_axis=0, concat_axis=0, tiled=True)  97.9 us
    all_to_all x1, waiting for transfers between devices, on_device(): lax.all_to_all(part, 'dict', split_axis=0, concat_axis=0, tiled=True)  94 us
    psum x1, waiting for transfers between devices, on_device(): dact = lax.psum(dact_local, 'dp')  91.8 us
  transfers between devices with their start and end apart: 3, of which 3 were waited for; matrix products, arithmetic and copies ran while one was open for 2% of the time, Pallas kernels for 0%

commit v1 on v0

v1 whole, which is shorter than its diff:
```python
import functools

import jax
import jax.numpy as jnp
from jax import lax
from jax.experimental import pallas as pl
from jax.experimental.pallas import tpu as pltpu
from jax.sharding import PartitionSpec as P

F32 = jnp.float32
BF16 = jnp.bfloat16
MESH = pl.DeviceIdType.MESH
VMEM_LIMIT = 60 * 2**20


def chip_at(k, z, nz):
    near = jnp.minimum(z, nz - 1 - z)
    odd = lax.rem(k, 2) == 1
    both = jnp.where(odd, z - (k + 1) // 2, z + k // 2)
    one = jnp.where(z <= nz - 1 - z, k, nz - 1 - k)
    return jnp.where(k <= 2 * near, both, one)


def remote(src, dst, send, recv, where):
    return pltpu.make_async_remote_copy(
        src_ref=src, dst_ref=dst, send_sem=send, recv_sem=recv,
        device_id=where, device_id_type=MESH,
    )


def greet(partners):
    barrier = pltpu.get_barrier_semaphore()
    for here, where in partners:
        @pl.when(here)
        def _():
            pl.semaphore_signal(barrier, inc=1, device_id=where, device_id_type=MESH)
    total = sum(jnp.where(here, 1, 0) for here, _ in partners)
    pl.semaphore_wait(barrier, total)


def gather_kernel(
    backward, nz, cap, rowb,
    pick_ref, shard_ref, w_ref, extra_ref, valid_ref,
    *refs,
):
    if backward:
        (rows_ref, out_ref, x_all, s1, r1, s2, r2, acc_ref, rsem, right_sem, left_sem,
         sib_sem, s1_sem, r1_sem, s2_sem, r2_sem) = refs
    else:
        (rows_ref, acc_ref, out_ref, x_all, s1, r1, s2, r2, rsem, right_sem, left_sem,
         sib_sem, s1_sem, r1_sem, s2_sem, r2_sem) = refs
    d = lax.axis_index("dp")
    me = lax.axis_index("dict")
    z, c = me // 2, lax.rem(me, 2)
    home_rows = shard_ref.shape[0]
    unit = 2 * cap * rowb
    half = s1.shape[2]
    right, left, sib = (d, me + 2), (d, me - 2), (d, me + 1 - 2 * c)
    d1 = d + 1 - 2 * lax.rem(d, 2)
    d2 = d + 2 - 4 * (d // 2)
    firsts, seconds = ((d1, me), (d2, me)), ((d2, me), (d1, me))
    true = me >= 0
    greet([(z < nz - 1, right), (z > 0, left), (true, sib), (true, (d1, me)), (true, (d2, me))])

    def span(h):
        return x_all.at[pl.ds(pl.multiple_of(h * home_rows, home_rows), home_rows)]

    def to(h, sems, where):
        return remote(span(h), span(h), sems.at[h], rsem.at[h], where)

    def forward(h, chip):
        @pl.when((chip <= z) & (z < nz - 1))
        def _():
            to(h, right_sem, right).start()

        @pl.when((chip >= z) & (z > 0))
        def _():
            to(h, left_sem, left).start()

        to(h, sib_sem, sib).start()

    def unit_rows(chip):
        return pl.ds(pl.multiple_of(chip * unit, unit), unit)

    def swap(src, dst, send, recv, part, chip, partners):
        at = unit_rows(chip)
        return remote(
            src.at[part, at], dst.at[part, at], send.at[part, chip], recv.at[part, chip],
            partners[part],
        )

    x_all[pl.ds(pl.multiple_of(me * home_rows, home_rows), home_rows), :] = shard_ref[...]

    def step(k, carry):
        @pl.when(k < nz)
        def _():
            chip = chip_at(k, z, nz)
            mine, other = 2 * chip + c, 2 * chip + 1 - c

            @pl.when(k > 0)
            def _():
                to(mine, sib_sem, sib).wait_recv()

            forward(mine, chip)
            to(other, sib_sem, sib).wait_recv()
            for core in range(2):
                h = 2 * chip + core
                home = pl.ds(pl.multiple_of(h * home_rows, home_rows), home_rows)
                slots = pl.ds(pl.multiple_of(h * cap * rowb, cap * rowb), cap * rowb)
                width = min(512, x_all.shape[1])
                for lo in range(0, x_all.shape[1], width):
                    rows_ref[slots, lo:lo + width] = jnp.dot(
                        pick_ref[h], x_all[home, lo:lo + width], preferred_element_type=F32
                    ).astype(BF16)
            at = unit_rows(chip)
            for part in range(2):
                for piece in range(2):
                    width = half // 2
                    lo = part * half + piece * width
                    if backward:
                        got = lax.dot_general(
                            rows_ref[at, :], w_ref[lo:lo + width, :], (((1,), (1,)), ((), ())),
                            preferred_element_type=F32,
                        )
                    else:
                        got = jnp.dot(
                            rows_ref[at, :], w_ref[:, lo:lo + width], preferred_element_type=F32
                        )
                    acc_ref[at, lo:lo + width] = got
                    s1[part, at, piece * width:(piece + 1) * width] = got.astype(BF16)
                swap(s1, r1, s1_sem, r1_sem, part, chip, firsts).start()

        @pl.when((k >= 1) & (k <= nz))
        def _():
            chip = chip_at(k - 1, z, nz)
            at = unit_rows(chip)
            for part in range(2):
                swap(s1, r1, s1_sem, r1_sem, part, chip, firsts).wait()
                lo = part * half
                got = acc_ref[at, lo:lo + half] + r1[part, at, :].astype(F32)
                acc_ref[at, lo:lo + half] = got
                s2[part, at, :] = got.astype(BF16)
                swap(s2, r2, s2_sem, r2_sem, part, chip, seconds).start()

        @pl.when(k >= 2)
        def _():
            chip = chip_at(k - 2, z, nz)
            at = unit_rows(chip)
            for part in range(2):
                swap(s2, r2, s2_sem, r2_sem, part, chip, seconds).wait()
                lo = part * half
                got = acc_ref[at, lo:lo + half] + r2[part, at, :].astype(F32)
                if backward:
                    out_ref[at, lo:lo + half] = (
                        got * 2.0 * extra_ref[at, lo:lo + half]
                    ).astype(BF16)
                else:
                    got = got + extra_ref[:, lo:lo + half].astype(F32)
                    got = jnp.where(valid_ref[at, :] > 0, jnp.maximum(got, 0.0), 0.0)
                    acc_ref[at, lo:lo + half] = got
                    out_ref[at, lo:lo + half] = (got * got).astype(BF16)
        return carry

    lax.fori_loop(0, nz + 2, step, 0)

    def drain(chip, carry):
        h = 2 * chip + c

        @pl.when((chip <= z) & (z < nz - 1))
        def _():
            to(h, right_sem, right).wait_send()

        @pl.when((chip >= z) & (z > 0))
        def _():
            to(h, left_sem, left).wait_send()

        to(h, sib_sem, sib).wait_send()
        return carry

    lax.fori_loop(0, nz, drain, 0)


def gather(backward, peers, cap, rowb, collective_id, pick, shard, w, extra, valid):
    nz = peers // 2
    total = peers * cap * rowb
    features = shard.shape[1]
    panel = w.shape[0] if backward else w.shape[1]
    vmem = pl.BlockSpec(memory_space=pltpu.VMEM)
    rows = jax.ShapeDtypeStruct((total, features), BF16)
    low = jax.ShapeDtypeStruct((total, panel), BF16)
    wide = jax.ShapeDtypeStruct((total, panel), F32)
    swap = pltpu.VMEM((2, total, panel // 2), BF16)
    dma = pltpu.SemaphoreType.DMA
    return pl.pallas_call(
        functools.partial(gather_kernel, backward, nz, cap, rowb),
        out_shape=(rows, low) if backward else (rows, wide, low),
        in_specs=[vmem] * 5,
        out_specs=(vmem,) * (2 if backward else 3),
        scratch_shapes=[pltpu.VMEM((peers * shard.shape[0], features), BF16)]
        + [swap] * 4
        + ([pltpu.VMEM((total, panel), F32)] if backward else [])
        + [dma((peers,))] * 4
        + [dma((2, nz))] * 4,
        compiler_params=pltpu.CompilerParams(
            collective_id=collective_id, has_side_effects=True, vmem_limit_bytes=VMEM_LIMIT
        ),
        cost_estimate=pl.CostEstimate(
            flops=2 * total * features * panel, bytes_accessed=20 * 2**20, transcendentals=0
        ),
    )(pick, shard, w, extra, valid)


def reduce_kernel(
    nz, cap, rowb,
    place_ref, act_ref, w_ref, shard_ref, bias_ref,
    out_ref, dense, sib_in, acc, line_in,
    sib_send, sib_recv, line_send, line_recv,
):
    d = lax.axis_index("dp")
    me = lax.axis_index("dict")
    z, c = me // 2, lax.rem(me, 2)
    home_rows, features = shard_ref.shape
    slots = cap * rowb
    right, left, sib = (d, me + 2), (d, me - 2), (d, me + 1 - 2 * c)
    true = me >= 0
    greet([(z < nz - 1, right), (z > 0, left), (true, sib)])
    def spread(h, target):
        at = pl.ds(pl.multiple_of(h * slots, slots), slots)
        width = min(512, features)
        for lo in range(0, features, width):
            part = jnp.dot(
                act_ref[at, :], w_ref[:, lo:lo + width], preferred_element_type=F32
            ).astype(BF16)
            target[:, lo:lo + width] = jnp.dot(
                place_ref[h], part, preferred_element_type=F32
            ).astype(BF16)

    def to_sib(chip):
        return remote(dense.at[chip], sib_in.at[chip], sib_send.at[chip], sib_recv.at[chip], sib)

    def along(chip, slot, where):
        return remote(acc.at[chip], line_in.at[slot], line_send.at[chip], line_recv.at[slot], where)

    def step(i, carry):
        chip = chip_at(nz - 1 - i, z, nz)
        spread(2 * chip + 1 - c, dense.at[chip])
        to_sib(chip).start()
        spread(2 * chip + c, acc.at[chip])
        to_sib(chip).wait_recv()

        @pl.when(chip != z)
        def _():
            behind = jnp.where(chip > z, z > 0, z < nz - 1)

            @pl.when(behind)
            def _():
                along(chip, chip, left).wait_recv()
                acc[chip] = (
                    acc[chip].astype(F32) + sib_in[chip].astype(F32) + line_in[chip].astype(F32)
                ).astype(BF16)

            @pl.when(jnp.logical_not(behind))
            def _():
                acc[chip] = (acc[chip].astype(F32) + sib_in[chip].astype(F32)).astype(BF16)

            @pl.when(chip > z)
            def _():
                along(chip, chip, right).start()

            @pl.when(chip < z)
            def _():
                slot = jnp.where(chip == z - 1, nz, chip)
                along(chip, slot, left).start()

        return carry

    lax.fori_loop(0, nz, step, 0)
    bias = bias_ref[...].astype(F32) - shard_ref[...].astype(F32)
    out_ref[...] = acc[z].astype(F32) + sib_in[z].astype(F32) + bias

    @pl.when(z > 0)
    def _():
        along(z, z, right).wait_recv()
        out_ref[...] = out_ref[...] + line_in[z].astype(F32)

    @pl.when(z < nz - 1)
    def _():
        along(z, nz, right).wait_recv()
        out_ref[...] = out_ref[...] + line_in[nz].astype(F32)

    def drain(chip, carry):
        to_sib(chip).wait_send()

        @pl.when(chip != z)
        def _():
            along(chip, chip, right).wait_send()

        return carry

    lax.fori_loop(0, nz, drain, 0)


def reduce(peers, cap, rowb, collective_id, place, act, w, shard, bias):
    nz = peers // 2
    home_rows, features = shard.shape
    vmem = pl.BlockSpec(memory_space=pltpu.VMEM)
    dma = pltpu.SemaphoreType.DMA
    one = (home_rows, features)
    return pl.pallas_call(
        functools.partial(reduce_kernel, nz, cap, rowb),
        out_shape=jax.ShapeDtypeStruct(one, F32),
        in_specs=[vmem] * 5,
        out_specs=vmem,
        scratch_shapes=[
            pltpu.VMEM((nz, *one), BF16),
            pltpu.VMEM((nz, *one), BF16),
            pltpu.VMEM((nz, *one), BF16),
            pltpu.VMEM((nz + 1, *one), BF16),
            dma((nz,)), dma((nz,)), dma((nz,)), dma((nz + 1,)),
        ],
        compiler_params=pltpu.CompilerParams(
            collective_id=collective_id, has_side_effects=True, vmem_limit_bytes=VMEM_LIMIT
        ),
        cost_estimate=pl.CostEstimate(
            flops=2 * act.shape[0] * act.shape[1] * features,
            bytes_accessed=8 * 2**20, transcendentals=0,
        ),
    )(place, act, w, shard, bias)


def on_device(acts, lists, w_enc, w_dec, b_enc, b_dec):
    peers = lax.axis_size("dict")
    me = lax.axis_index("dict")
    blocks, active = lists.shape
    rowb = acts.shape[0] // blocks
    features = acts.shape[1]
    cap = max(2, (2 * blocks * active + peers - 1) // peers)
    everyone = lax.all_gather(lists, "dict", axis=0)
    member = jnp.any(everyone == me, axis=2)
    count = member.astype(jnp.int32)
    ids = jnp.arange(blocks, dtype=jnp.int32)
    before = (ids[:, None] > ids[None, :]).astype(jnp.int32)
    rank = jnp.sum(count[:, None, :] * before[None], axis=2)
    place = jnp.where(member, rank, cap)
    match = place[:, None, :] == jnp.arange(cap, dtype=jnp.int32)[None, :, None]
    slots = jnp.sum(jnp.where(match, ids[None, None, :] + 1, 0), axis=2) - 1
    slots = jnp.repeat(slots, rowb, axis=1)
    offset = jnp.arange(cap * rowb, dtype=jnp.int32) % rowb
    source = jnp.where(slots >= 0, slots * rowb + offset[None, :], -1)
    columns = jnp.arange(acts.shape[0], dtype=jnp.int32)
    pick = (source[:, :, None] == columns[None, None, :]).astype(BF16)
    put = (columns[None, :, None] == source[:, None, :]).astype(BF16)
    valid = (source >= 0).astype(F32).reshape(-1, 1)

    rows_in, relu, act = gather(
        False, peers, cap, rowb, 0, pick, acts, w_enc, b_enc[None, :], valid
    )
    calls = max(1, peers // 8)
    width = features // calls
    pieces = []
    for i in range(calls):
        cols = slice(i * width, (i + 1) * width)
        diff = reduce(
            peers, cap, rowb, 2 + i, put, act, w_dec[:, cols], acts[:, cols], b_dec[None, cols]
        )
        pieces.append((diff * (1.0 / rowb)).astype(BF16))
    residual = pieces[0] if calls == 1 else jnp.concatenate(pieces, axis=1)
    resid_in, grad_pre = gather(
        True, peers, cap, rowb, 1, pick, residual, w_dec, relu, valid
    )
    first_rows = (((0,), (0,)), ((), ()))
    grad_dec = lax.dot_general(act, resid_in, first_rows, preferred_element_type=F32).astype(BF16)
    grad_enc = lax.dot_general(rows_in, grad_pre, first_rows, preferred_element_type=F32).astype(BF16)
    return grad_enc, grad_dec


def solution(mesh):
    in_specs = (
        P("dict", "dp"),
        P("dict", None),
        P("dp", "dict"),
        P("dict", "dp"),
        P("dict"),
        P("dp"),
    )
    out_specs = (P("dp", "dict"), P("dict", "dp"))
    return jax.shard_map(
        on_device, mesh=mesh, in_specs=in_specs, out_specs=out_specs, check_vma=False
    )
```

time: 595 us -> 345 us (0.58)
  Pallas kernels: 0 us -> 305 us
  waiting for transfers between devices: 288 us -> 0 us
  blocking collectives: 199 us -> 13.7 us
  matrix products: 54.5 us -> 15.8 us
  local copies, waits for them, and re-layouts: 32.4 us -> 3.74 us
  between operations: 14.1 us -> 0.77 us
    pallas_call x0 -> x3, Pallas kernels: none -> 305 us  [the longest x2 219 us: gather(): pl.pallas_call(functools.partial(gather_kernel, backward, nz, cap, rowb),...]
    all_to_all x2 -> x0, blocking collectives: 199 us -> none  [the longest x1 101 us: on_device(): lax.all_to_all(outgoing, 'dict', split_axis=0, concat_axis=0, tiled=True)]
    psum x2 -> x0, waiting for transfers between devices: 194 us -> none  [the longest x1 102 us: on_device(): preact = lax.psum(pre_local, 'dp') + bias_enc]
    all_to_all x1 -> x0, waiting for transfers between devices: 94 us -> none  [on_device(): lax.all_to_all(part, 'dict', split_axis=0, concat_axis=0, tiled=True)]
    dot_general x9 -> x2, matrix products: 54.5 us -> 15.8 us  [the longest x1 9.59 us: on_device(): lax.dot_general(rows_in, grad_pre, first_rows, preferred_element_type=F32)]
    reshape x7 -> x0, local copies, waits for them, and re-layouts: 27 us -> none  [the longest x1 7.37 us: on_device(): returned = returned.reshape(slot_total, rows_block * feature_cols)]
    all_gather x0 -> x1, blocking collectives: none -> 13.7 us  [on_device(): everyone = lax.all_gather(lists, 'dict', axis=0)]
  transfers between devices with their start and end apart: 3 -> 0, of which waited for: 3 -> 0; matrix products, arithmetic and copies ran while one was open for 2% -> 0% of each run, Pallas kernels for 0% -> 0%
where the time goes in v1:
time: 345 us
  Pallas kernels  305 us (88%)
  matrix products  15.8 us (5%)
  blocking collectives  13.7 us (4%)
  other arithmetic  6.03 us (2%)
  local copies, waits for them, and re-layouts  3.74 us (1%)
    pallas_call x2, Pallas kernels, gather(): pl.pallas_call(functools.partial(gather_kernel, backward, nz, cap, rowb),...  219 us
    pallas_call x1, Pallas kernels, reduce(): pl.pallas_call(functools.partial(reduce_kernel, nz, cap, rowb), out_shape...  85.5 us
    all_gather x1, blocking collectives, on_device(): everyone = lax.all_gather(lists, 'dict', axis=0)  13.7 us
    dot_general x1, matrix products, on_device(): lax.dot_general(rows_in, grad_pre, first_rows, preferred_element_type=F32)  9.59 us

profile of v1, /device:TPU:0, one launch (start us, length us, event | category | flops | bytes accessed | tf_op | source)
XLA Modules:
  0.0 344.7 jit_solution(9310403901237472636)
XLA Ops:
  0.7 1.3 broadcast_in_dim.51.extra_ref
  1.9 13.7 %all-gather.1 = s32[8,16,2]{1,2,0:T(2,128)S(1)} all-gather(s32[1,16,2]{1,2,0:T(2,128)} %bitcast.7), channel_id=2, replica_groups=mesh['dp'=4,'dict'=8] {'dict'}, dimensions={0}, use_global_device_ids=true | all-gather | bytes 1152 | tf_op jit(solution)/shard_map/all_gather | solution.py:338
  15.6 1.3 broadcast_in_dim.53.bias_ref
  16.9 0.2 multiply_reduce_fusion
  17.2 0.2 select_reduce_fusion
  17.4 0.1 broadcast_in_dim.48
  17.5 0.1 ge.37
  17.6 0.1 broadcast_in_dim.49
  17.6 0.1 mul.53
  17.7 0.3 ge.40
  18.1 0.3 mul.57
  18.4 0.2 copy.15
  18.6 0.9 fusion.2.valid_ref
  19.5 1.0 fusion.pick_ref
  20.5 0.9 fusion.1.place_ref
  21.4 109.4 %shard_map.77 = (bf16[1024,2048]{1,0:T(8,128)(2,1)}, f32[1024,1024]{1,0:T(8,128)}, bf16[1024,1024]{1,0:T(8,128)(2,1)}) custom-call(bf16[8,128,256]{2,1,0:T(8,128)(2,1)} %fusion.pick_ref, bf16[256,2048]{1,0:T(8,128)(2,1)} %shard_ref.3, bf16[2048,1024]{1,0:T(8,128)(2,1)} %w_ref.3, bf16[1,1024]{1,0:T(2,128)(2,1)} %broadcast_in_dim.51.extra_ref, ...), custom_call_target="tpu_custom_call" | custom-call | flops 4294967296 | bytes 20971520 | tf_op jit(solution)/shard_map/pallas_call | solution.py:194
  130.8 85.5 %shard_map.78 = f32[256,2048]{1,0:T(8,128)} custom-call(bf16[8,256,128]{2,1,0:T(8,128)(2,1)} %fusion.1.place_ref, bf16[1024,1024]{1,0:T(8,128)(2,1)} %get-tuple-element.8.act_ref, bf16[1024,2048]{1,0:T(8,128)(2,1)} %w_ref.5, bf16[256,2048]{1,0:T(8,128)(2,1)} %shard_ref.3, bf16[1,2048]{1,0:T(2,128)(2,1)} %broadcast_in_dim.53.bias_ref), custom_call_target="tpu_custom_call" | custom-call | flops 4294967296 | bytes 8388608 | tf_op jit(solution)/shard_map/pallas_call | solution.py:309
  216.3 2.7 multiply_convert_fusion.shard_ref
  219.0 109.8 %shard_map.79 = (bf16[1024,2048]{1,0:T(8,128)(2,1)}, bf16[1024,1024]{1,0:T(8,128)(2,1)}) custom-call(bf16[8,128,256]{2,1,0:T(8,128)(2,1)} %fusion.pick_ref, bf16[256,2048]{1,0:T(8,128)(2,1)} %multiply_convert_fusion.shard_ref, bf16[1024,2048]{1,0:T(8,128)(2,1)} %w_ref.5, f32[1024,1024]{1,0:T(8,128)} %get-tuple-element.9.extra_ref, f32[1024,1]{1,0:T(8,128)} %fusion.2.valid_ref), custom_call_target="tpu_custom_call" | custom-call | flops 4294967296 | bytes 20971520 | tf_op jit(solution)/shard_map/pallas_call | solution.py:194
  328.8 0.0 copy-start
  328.8 0.0 copy-start.1
  328.8 9.6 %convolution_convert_fusion.1 = bf16[2048,1024]{1,0:T(8,128)(2,1)} fusion(bf16[1024,2048]{1,0:T(8,128)(2,1)} %get-tuple-element.7, bf16[1024,1024]{1,0:T(8,128)(2,1)} %get-tuple-element.10), kind=kOutput, calls=%fused_computation.1 | convolution fusion | flops 4297064448 | bytes 10485760 | tf_op jit(solution)/shard_map/dot_general | solution.py:373
  338.4 0.0 copy-done
  338.4 0.0 copy-done.1
  338.4 6.2 %convolution_convert_fusion = bf16[1024,2048]{1,0:T(8,128)(2,1)} fusion(bf16[1024,1024]{1,0:T(8,128)(2,1)S(1)} %copy-done.1, bf16[1024,2048]{1,0:T(8,128)(2,1)S(1)} %copy-done), kind=kOutput, calls=%fused_computation | convolution fusion | flops 4297064448 | bytes 10485760 | tf_op jit(solution)/shard_map/dot_general | solution.py:372
  (10 shorter events, 0.1 us)
Async XLA Ops:
  328.8 9.6 %copy-start = (bf16[1024,2048]{1,0:T(8,128)(2,1)S(1)}, bf16[1024,2048]{1,0:T(8,128)(2,1)}, u32[]{:S(2)}) copy-start(bf16[1024,2048]{1,0:T(8,128)(2,1)} %get-tuple-element.11) | copy-start | bytes 12582916
  328.8 9.6 %copy-start.1 = (bf16[1024,1024]{1,0:T(8,128)(2,1)S(1)}, bf16[1024,1024]{1,0:T(8,128)(2,1)}, u32[]{:S(2)}) copy-start(bf16[1024,1024]{1,0:T(8,128)(2,1)} %get-tuple-element.8.act_ref) | copy-start | bytes 6291460
